TPU v7x, 32 devices: a whole 2x2x4 slice. The times are simulated.
32 devices in a mesh: groups: 2 (over y), store: 4 (over z), layer: 4 (over x, core).
Axes of the slice: x: 2, y: 2, z: 4, core: 2. Of those that a mesh axis runs over, the one named last changes fastest.
Arguments:
- query_inputs: bfloat16 [4, 256, 2, 4096], P('layer', ('groups', 'store')), parts along dimension 1, may hold values from -6 to 6
- query_grads: bfloat16 [4, 256, 2, 4096], P('layer', ('groups', 'store')), parts along dimension 1
- proj_in: bfloat16 [4, 64, 4096], P('layer')
- proj_out: bfloat16 [4, 32, 4096], P('layer'), may hold values from -0.09375 to 0.09375
- hess_inv: bfloat16 [4, 16, 128, 128], P('layer'), as said below
- store_sketch: bfloat16 [5888, 8192], P(('groups', 'store'), 'layer'), parts along dimension 0, may hold values from -6 to 6
Outputs:
- scores: bfloat16 [256, 2944], P(('groups', 'layer'), 'store'), parts along dimension 0
There are 2 independent parts, one for each index of `groups`. A program takes and returns all parts, laid end to end along the dimension named above; an argument that names none is the same for every part. Nothing has to cross between parts.
Inputs may be any that keep to these rules, and one draw needn't show every extreme that they name: `hess_inv`: each 128 x 128 block is symmetric and positive definite.
All inputs are finite; a program needn't handle non-finite values.
Results may differ from a plain program's by a relative error of at most 0.012.
Values may be sent and summed in bfloat16 or wider, within the bound.
A program may use at most 64 MiB of HBM per device.

v0:
```python
import jax
import jax.numpy as jnp
from jax import lax
from jax.sharding import PartitionSpec as P

epsilon = 1e-06


def shards(query_inputs, query_grads, proj_in, proj_out, hess_inv, store_sketch):
    inputs = query_inputs[0]
    gradients = query_grads[0]
    projected_in = jnp.einsum("qtd,kd->qtk", inputs, proj_in[0], preferred_element_type=jnp.float32)
    projected_out = jnp.einsum(
        "qtd,od->qto", gradients, proj_out[0], preferred_element_type=jnp.float32
    )
    outer_sum = jnp.einsum(
        "qto,qtk->qok", projected_out, projected_in, precision=lax.Precision.HIGHEST
    )
    query_count = outer_sum.shape[0]
    blocks = hess_inv.shape[1]
    block_size = hess_inv.shape[2]
    blocked = outer_sum.reshape(query_count, blocks, block_size).astype(jnp.bfloat16)
    precond = jnp.einsum("qbj,bij->qbi", blocked, hess_inv[0], preferred_element_type=jnp.float32)
    precond = precond.reshape(query_count, blocks * block_size)
    partial_squares = jnp.sum(precond * precond, axis=1)
    total_squares = lax.psum(partial_squares, "layer")
    normed = (precond * lax.rsqrt(total_squares + epsilon)[:, None]).astype(jnp.bfloat16)
    all_rows = query_count * lax.axis_size("store")
    own_rows = all_rows // lax.axis_size("layer")
    partial_value = lax.dot_general(
        lax.all_gather(normed, "store", axis=0, tiled=True),
        store_sketch,
        (((1,), (1,)), ((), ())),
        preferred_element_type=jnp.float32,
    )
    summed = lax.psum(partial_value.astype(jnp.bfloat16), "layer").astype(jnp.float32)
    own_scores = lax.dynamic_slice_in_dim(summed, lax.axis_index("layer") * own_rows, own_rows, 0)
    return own_scores.astype(jnp.bfloat16)


def solution(mesh):
    return jax.shard_map(
        shards,
        mesh=mesh,
        in_specs=(
            P("layer", ("groups", "store"), None, None),
            P("layer", ("groups", "store"), None, None),
            P("layer", None, None),
            P("layer", None, None),
            P("layer", None, None, None),
            P(("groups", "store"), "layer"),
        ),
        out_specs=P(("groups", "layer"), "store"),
        check_vma=False,
    )
```

profile of v0, /device:TPU:0, one launch (start us, length us, event | category | flops | bytes accessed | tf_op | source)
XLA Modules:
  0.0 79.7 jit_solution(12914489585912699733)
XLA Ops:
  6.5 0.0 copy-start
  6.5 0.0 all-reduce.2.cloned.1.call-start
  6.5 1.8 %fusion.2 = f32[32,2,64]{2,0,1:T(8,128)S(1)} fusion(bf16[1,64,4096]{2,1,0:T(8,128)(2,1)} %param.8, bf16[32,2,4096]{2,1,0:T(2,128)(2,1)} %bitcast.28), kind=kOutput, calls=%fused_computation.4 | convolution fusion | flops 33554432 | bytes 1064960 | tf_op jit(solution)/shard_map/qtd,kd->qtk/dot_general | solution.py:12
  8.4 1.6 %fusion.5 = f32[32,2,32]{2,0,1:T(8,128)S(1)} fusion(bf16[32,2,4096]{2,1,0:T(2,128)(2,1)} %bitcast.29, bf16[1,32,4096]{2,1,0:T(8,128)(2,1)} %param.9), kind=kOutput, calls=%fused_computation.7 | convolution fusion | flops 16777216 | bytes 794624 | tf_op jit(solution)/shard_map/qtd,od->qto/dot_general | solution.py:13
  10.0 1.0 %convolution_convert_fusion = bf16[32,32,64]{2,1,0:T(8,128)(2,1)S(1)} fusion(f32[32,2,64]{2,0,1:T(8,128)S(1)} %fusion.2, f32[32,2,32]{2,0,1:T(8,128)S(1)} %fusion.5), kind=kOutput, calls=%fused_computation | convolution fusion | flops 1638400 | bytes 155648 | tf_op jit(solution)/shard_map/qto,qtk->qok/dot_general | solution.py:16
  11.0 0.1 convert_element_type.19
  11.2 1.5 %fusion.8 = (f32[32]{0:T(128)S(1)}, f32[16,32,128]{2,1,0:T(8,128)S(1)}) fusion(bf16[1,16,128,128]{3,2,1,0:T(8,128)(2,1)} %param.10, bf16[32,16,128]{2,1,0:T(8,128)(2,1)S(1)} %convert_element_type.19), kind=kOutput, calls=%fused_computation.12 | convolution fusion | flops 16908256 | bytes 917632 | tf_op jit(solution)/shard_map/qbj,bij->qbi/dot_general | solution.py:23
  12.7 8.3 %psum.14 = f32[32]{0:T(128)S(1)} all-reduce(f32[32]{0:T(128)S(1)} %get-tuple-element.5), channel_id=1, replica_groups=mesh['groups'=2,'store'=4,'layer'=4] {'layer'}, use_global_device_ids=true, to_apply=%region_1.0 | all-reduce | flops 32 | bytes 256 | tf_op jit(solution)/shard_map/psum | solution.py:26
  21.0 0.1 fusion.7
  21.1 15.5 %all_gather.3 = bf16[128,2048]{1,0:T(8,128)(2,1)S(1)} all-gather(bf16[32,2048]{1,0:T(8,128)(2,1)S(1)} %fusion.7), channel_id=1, replica_groups=mesh['groups'=2,'store'=4,'layer'=4] {'store'}, dimensions={0}, use_global_device_ids=true | all-gather | bytes 655360 | tf_op jit(solution)/shard_map/all_gather | solution.py:31
  36.6 0.0 copy-done
  36.6 1.8 %convolution_convert_fusion.1 = bf16[128,736]{1,0:T(8,128)(2,1)} fusion(bf16[128,2048]{1,0:T(8,128)(2,1)S(1)} %all_gather.3, bf16[736,2048]{1,0:T(8,128)(2,1)S(1)} %copy-done), kind=kOutput, calls=%fused_computation.1 | convolution fusion | flops 385970176 | bytes 3727360 | tf_op jit(solution)/shard_map/dot_general | solution.py:30
  38.4 0.0 all-reduce.2.cloned.1.call-update
  38.4 33.0 %all-reduce.2.cloned.1.call-done = bf16[128,736]{1,0:T(8,128)(2,1)} async-done(((bf16[128,736]{1,0:T(8,128)(2,1)}), bf16[128,736]{1,0:T(8,128)(2,1)}) %all-reduce.2.cloned.1.call-update) | async-done | bytes 188432 | tf_op jit(solution)/shard_map/psum | solution.py:36
  71.4 1.4 %convert_convert_fusion = bf16[32,736]{1,0:T(8,128)(2,1)} fusion(bf16[128,736]{1,0:T(8,128)(2,1)} %all-reduce.2.cloned.1.call-done, s32[]{:T(128)S(6)} %select_n.3), kind=kLoop, calls=%fused_computation.15 | loop fusion | flops 47104 | bytes 94212 | tf_op jit(solution)/shard_map/convert_element_type | solution.py:38
  (1 shorter events, 0.0 us)
Async XLA Ops:
  6.5 30.1 %copy-start = (bf16[736,2048]{1,0:T(8,128)(2,1)S(1)}, bf16[736,2048]{1,0:T(8,128)(2,1)}, u32[]{:S(2)}) copy-start(bf16[736,2048]{1,0:T(8,128)(2,1)} %param.11) | copy-start | bytes 9043972
  6.5 64.9 %all-reduce.2.cloned.1.call-start = ((), (), s32[]{:S(2)}) async-start(), calls=%async_computation | async-start | bytes 393216 | tf_op jit(solution)/shard_map/psum | solution.py:36
Sparse Core Ops, SparseCore 0:
  38.5 32.8 all-reduce.1
where the time goes:
time: 79.9 us; the launch traced here: 79.7 us
  waiting for transfers between devices  33 us (41%)
  blocking collectives  23.8 us (30%)
  between operations  13.4 us (17%)
  matrix products  7.73 us (10%)
  other arithmetic  1.52 us (2%)
    psum x1, waiting for transfers between devices, shards(): lax.psum(partial_value.astype(jnp.bfloat16), 'layer').astype(jnp.float32)  33 us
    all_gather x1, blocking collectives, shards(): lax.all_gather(normed, 'store', axis=0, tiled=True)  15.5 us
    psum x1, blocking collectives, shards(): total_squares = lax.psum(partial_squares, 'layer')  8.34 us
    dot_general x1, matrix products, shards(): jnp.einsum('qtd,kd->qtk', inputs, proj_in[0], preferred_element_type=jnp....  1.84 us
    dot_general x1, matrix products, shards(): lax.dot_general(lax.all_gather(normed, 'store', axis=0, tiled=True), stor...  1.76 us
  transfers between devices with their start and end apart: 1, of which 1 were waited for; matrix products, arithmetic and copies ran while one was open for 0% of the time, Pallas kernels for 0%

commit v1 on v0

v1 whole, which is shorter than its diff:
```python
import functools

import jax
import jax.numpy as jnp
from jax import lax
from jax.experimental import pallas as pl
from jax.experimental.pallas import tpu as pltpu
from jax.sharding import PartitionSpec as P

epsilon = 1e-06
MESH = pl.DeviceIdType.MESH
CHUNK = 256
LANES = 128
f32, bf16 = jnp.float32, jnp.bfloat16


def contract(a, b):
    return lax.dot_general(a, b, (((1,), (1,)), ((), ())), preferred_element_type=f32)


def repeat(count, body):
    if count == 1:
        body(0)
    else:
        lax.fori_loop(0, count, lambda i, _: (body(i), None)[1], None)


def kernel(
    stores, layers, peers_per_step,
    qin_hbm, qgr_hbm, pin_hbm, pout_hbm, hess_hbm, store_hbm, out_ref,
    qin, qgr, pin, pout, hess, store, mixed, factors, expand, unit, norms, part, got,
    load_sem, fsend_sem, frecv_sem, psend_sem, precv_sem,
):
    my_store, my_layer = lax.axis_index("store"), lax.axis_index("layer")
    queries, tokens, _ = qin.shape
    k_in, k_out = pin.shape[0], pout.shape[0]
    blocks, blk, _ = hess.shape
    rows = store_hbm.shape[0]
    chunks = part.shape[0]
    own = got.shape[2]
    tail = rows - (chunks - 1) * CHUNK

    def load(source, target, index):
        copy = pltpu.make_async_copy(source, target, load_sem.at[index])
        copy.start()
        return copy

    loads = [
        load(qin_hbm.at[0], qin, 0),
        load(pin_hbm.at[0], pin, 1),
        load(qgr_hbm.at[0], qgr, 2),
        load(pout_hbm.at[0], pout, 3),
        load(hess_hbm.at[0], hess, 4),
    ]
    store_loads = []
    for c in range(chunks):
        size = CHUNK if c < chunks - 1 else tail
        at = pl.ds(c * CHUNK, size)
        store_loads.append(load(store_hbm.at[at], store.at[at], 5 + c))

    barrier = pltpu.get_barrier_semaphore()
    for hop in range(1, stores):
        pl.semaphore_signal(
            barrier, inc=1, device_id={"store": lax.rem(my_store + hop, stores)}, device_id_type=MESH
        )
    for hop in range(1, layers):
        pl.semaphore_signal(
            barrier, inc=1, device_id={"layer": lax.rem(my_layer + hop, layers)}, device_id_type=MESH
        )

    depth = expand.shape[0]
    sketch = blocks * blk
    row = lax.rem(lax.broadcasted_iota(jnp.int32, (depth, LANES), 0), LANES)
    col = lax.broadcasted_iota(jnp.int32, (depth, LANES), 1)
    per_block = blk // k_in
    for b in range(blocks):
        hit = row == k_in + b * per_block + col // k_in
        expand[:, b * blk : (b + 1) * blk] = jnp.where(hit, 1.0, 0.0).astype(bf16)
    expand[:, sketch:] = jnp.where(row == lax.rem(col, k_in), 1.0, 0.0).astype(bf16)
    store[rows:, :] = jnp.zeros((chunks * CHUNK - rows, store.shape[1]), bf16)
    mixed[...] = jnp.zeros_like(mixed)

    loads[0].wait()
    loads[1].wait()
    mixed[:, 0:k_in] = contract(qin[...].reshape(queries * tokens, -1), pin[...])
    loads[2].wait()
    loads[3].wait()
    mixed[:, k_in : k_in + k_out] = contract(qgr[...].reshape(queries * tokens, -1), pout[...])
    for t in range(tokens):
        value = mixed[pl.ds(t, queries, stride=tokens), :]
        high = value.astype(bf16)
        factors[my_store, t * queries : (t + 1) * queries, 0:LANES] = high
        factors[my_store, t * queries : (t + 1) * queries, LANES:] = (
            value - high.astype(f32)
        ).astype(bf16)

    pl.semaphore_wait(barrier, stores + layers - 2)

    def factor_copy(hop):
        return pltpu.make_async_remote_copy(
            src_ref=factors.at[my_store],
            dst_ref=factors.at[my_store],
            send_sem=fsend_sem.at[hop - 1],
            recv_sem=frecv_sem.at[hop - 1],
            device_id={"store": lax.rem(my_store + hop, stores)},
            device_id_type=MESH,
        )

    def factor_arrival(hop):
        source = lax.rem(my_store - hop + stores, stores)
        return pltpu.make_async_remote_copy(
            src_ref=factors.at[source],
            dst_ref=factors.at[source],
            send_sem=fsend_sem.at[hop - 1],
            recv_sem=frecv_sem.at[hop - 1],
            device_id={"store": source},
            device_id_type=MESH,
        )

    for hop in range(1, stores):
        factor_copy(hop).start()
    loads[4].wait()
    for hop in range(1, stores):
        factor_arrival(hop).wait_recv()

    step_rows = peers_per_step * queries
    steps = stores // peers_per_step

    def precondition(step):
        at = pl.ds(step * peers_per_step, peers_per_step)
        joined = factors[at].reshape(peers_per_step * tokens * queries, depth)

        def spread(first):
            value = jnp.dot(joined, expand[:, first : first + blk], preferred_element_type=f32)
            return value.reshape(peers_per_step, tokens, queries, blk)

        features = spread(sketch)
        total = jnp.zeros((step_rows, blk), f32)
        to = pl.ds(pl.multiple_of(step * step_rows, step_rows), step_rows)
        for b in range(blocks):
            outer = jnp.sum(spread(b * blk) * features, axis=1)
            outer = outer.reshape(step_rows, blk).astype(bf16)
            precond = contract(outer, hess[b])
            total += precond * precond
            unit[to, b * blk : (b + 1) * blk] = precond.astype(bf16)
        norms[to, :] = jnp.broadcast_to(jnp.sum(total, axis=1, keepdims=True), (step_rows, LANES)) * 0.25

    repeat(steps, precondition)

    def part_copy(c, hop):
        peer = lax.rem(my_layer + hop, layers)
        return pltpu.make_async_remote_copy(
            src_ref=part.at[c, pl.ds(pl.multiple_of(peer * own, own), own)],
            dst_ref=got.at[c, hop - 1],
            send_sem=psend_sem.at[c, hop - 1],
            recv_sem=precv_sem.at[c, hop - 1],
            device_id={"layer": peer},
            device_id_type=MESH,
        )

    lane = lax.broadcasted_iota(jnp.int32, (step_rows, CHUNK), 1)
    for c in range(chunks):
        store_loads[c].wait()

        def score(step, c=c):
            to = pl.ds(pl.multiple_of(step * step_rows, step_rows), step_rows)
            value = contract(unit[to, :], store[c * CHUNK : (c + 1) * CHUNK, :])
            if c == chunks - 1:
                norm = norms[to, 0:1]
                high = norm.astype(bf16).astype(f32)
                value = jnp.where(lane == tail, high, value)
                value = jnp.where(lane == tail + 1, norm - high, value)
            part[c, to, :] = value.astype(bf16)

        repeat(steps, score)
        for hop in range(1, layers):
            part_copy(c, hop).start()

    mine = pl.ds(pl.multiple_of(my_layer * own, own), own)
    sums = []
    for c in range(chunks):
        value = part[c, mine, :].astype(f32)
        for hop in range(1, layers):
            part_copy(c, hop).wait_recv()
            value += got[c, hop - 1].astype(f32)
        sums.append(value)
    square = (sums[-1][:, tail : tail + 1] + sums[-1][:, tail + 1 : tail + 2]) * 4.0
    scale = lax.rsqrt(square + epsilon)
    for c in range(chunks):
        size = CHUNK if c < chunks - 1 else tail
        value = jnp.where(scale > 0.0, sums[c] * scale, 0.0).astype(bf16)
        out_ref[:, c * CHUNK : c * CHUNK + size] = value[:, :size]

    for hop in range(1, stores):
        factor_copy(hop).wait_send()
    for c in range(chunks):
        for hop in range(1, layers):
            part_copy(c, hop).wait_send()


def shards(stores, layers, query_inputs, query_grads, proj_in, proj_out, hess_inv, store_sketch):
    _, queries, tokens, width = query_inputs.shape
    k_in, k_out = proj_in.shape[1], proj_out.shape[1]
    _, blocks, blk, _ = hess_inv.shape
    rows, sketch = store_sketch.shape
    chunks = -(-(rows + 2) // CHUNK)
    every = queries * stores
    own = every // layers
    peers_per_step = 4 if stores % 4 == 0 else 1
    scratch = [
        pltpu.VMEM((queries, tokens, width), bf16),
        pltpu.VMEM((queries, tokens, width), bf16),
        pltpu.VMEM((k_in, width), bf16),
        pltpu.VMEM((k_out, width), bf16),
        pltpu.VMEM((blocks, blk, blk), bf16),
        pltpu.VMEM((chunks * CHUNK, sketch), bf16),
        pltpu.VMEM((tokens * queries, LANES), f32),
        pltpu.VMEM((stores, tokens * queries, 2 * LANES), bf16),
        pltpu.VMEM((2 * LANES, sketch + blk), bf16),
        pltpu.VMEM((every, sketch), bf16),
        pltpu.VMEM((every, LANES), f32),
        pltpu.VMEM((chunks, every, CHUNK), bf16),
        pltpu.VMEM((chunks, layers - 1, own, CHUNK), bf16),
        pltpu.SemaphoreType.DMA((5 + chunks,)),
        pltpu.SemaphoreType.DMA((stores - 1,)),
        pltpu.SemaphoreType.DMA((stores - 1,)),
        pltpu.SemaphoreType.DMA((chunks, layers - 1)),
        pltpu.SemaphoreType.DMA((chunks, layers - 1)),
    ]
    return pl.pallas_call(
        functools.partial(kernel, stores, layers, peers_per_step),
        out_shape=jax.ShapeDtypeStruct((own, rows), bf16),
        in_specs=[pl.BlockSpec(memory_space=pl.ANY)] * 6,
        out_specs=pl.BlockSpec(memory_space=pltpu.VMEM),
        scratch_shapes=scratch,
        compiler_params=pltpu.CompilerParams(
            collective_id=0, has_side_effects=True, vmem_limit_bytes=48 * 2**20
        ),
    )(query_inputs, query_grads, proj_in, proj_out, hess_inv, store_sketch)


def solution(mesh):
    return jax.shard_map(
        functools.partial(shards, mesh.shape["store"], mesh.shape["layer"]),
        mesh=mesh,
        in_specs=(
            P("layer", ("groups", "store"), None, None),
            P("layer", ("groups", "store"), None, None),
            P("layer", None, None),
            P("layer", None, None),
            P("layer", None, None, None),
            P(("groups", "store"), "layer"),
        ),
        out_specs=P(("groups", "layer"), "store"),
        check_vma=False,
    )
```

time: 79.9 us -> 25.7 us (0.32)
  waiting for transfers between devices: 33 us -> 0 us
  blocking collectives: 23.8 us -> 0 us
  Pallas kernels: 0 us -> 17.8 us
  between operations: 13.4 us -> 0.02 us
  matrix products: 7.73 us -> 0 us
  local copies, waits for them, and re-layouts: 0.15 us -> 7.59 us
  other arithmetic: 1.52 us -> 0 us
    psum x1 -> x0, waiting for transfers between devices: 33 us -> none  [shards(): lax.psum(partial_value.astype(jnp.bfloat16), 'layer').astype(jnp.float32)]
    pallas_call x0 -> x1, Pallas kernels: none -> 17.8 us  [shards(): pl.pallas_call(functools.partial(kernel, stores, layers, peers_per_step),...]
    all_gather x1 -> x0, blocking collectives: 15.5 us -> none  [shards(): lax.all_gather(normed, 'store', axis=0, tiled=True)]
    psum x1 -> x0, blocking collectives: 8.34 us -> none  [shards(): total_squares = lax.psum(partial_squares, 'layer')]
    dot_general x5 -> x0, matrix products: 7.73 us -> none  [the longest x1 1.84 us: shards(): jnp.einsum('qtd,kd->qtk', inputs, proj_in[0], preferred_element_type=jnp....]
    unnamed x2 -> x13, local copies, waits for them, and re-layouts: 0.01 us -> 7.59 us
    convert_element_type x2 -> x0, other arithmetic: 1.51 us -> none  [the longest x1 1.42 us: shards(): return own_scores.astype(jnp.bfloat16)]
  transfers between devices with their start and end apart: 1 -> 0, of which waited for: 1 -> 0; matrix products, arithmetic and copies ran while one was open for 0% -> 0% of each run, Pallas kernels for 0% -> 0%
where the time goes in v1:
time: 25.7 us; the launch traced here: 25.4 us
  Pallas kernels  17.8 us (69%)
  local copies, waits for them, and re-layouts  7.59 us (30%)
    pallas_call x1, Pallas kernels, shards(): pl.pallas_call(functools.partial(kernel, stores, layers, peers_per_step),...  17.8 us
    unnamed x13, local copies, waits for them, and re-layouts  7.59 us

profile of v1, /device:TPU:0, one launch (start us, length us, event | category | flops | bytes accessed | tf_op | source)
XLA Modules:
  0.0 25.4 jit_solution(17554351469918962866)
XLA Ops:
  0.0 0.0 copy-start
  0.0 1.9 %copy-done = bf16[736,2048]{1,0:T(8,128)(2,1)S(1)} copy-done((bf16[736,2048]{1,0:T(8,128)(2,1)S(1)}, bf16[736,2048]{1,0:T(8,128)(2,1)}, u32[]{:S(2)}) %copy-start) | copy-done | bytes 3014680
  1.9 0.0 copy-start.1
  1.9 1.0 %copy-done.1 = bf16[1,32,2,4096]{3,2,1,0:T(2,128)(2,1)S(1)} copy-done((bf16[1,32,2,4096]{3,2,1,0:T(2,128)(2,1)S(1)}, bf16[1,32,2,4096]{3,2,1,0:T(2,128)(2,1)}, u32[]{:S(2)}) %copy-start.1) | copy-done | bytes 524312
  2.9 0.0 copy-start.2
  2.9 1.0 %copy-done.2 = bf16[1,32,2,4096]{3,2,1,0:T(2,128)(2,1)S(1)} copy-done((bf16[1,32,2,4096]{3,2,1,0:T(2,128)(2,1)S(1)}, bf16[1,32,2,4096]{3,2,1,0:T(2,128)(2,1)}, u32[]{:S(2)}) %copy-start.2) | copy-done | bytes 524312
  3.9 0.0 copy-start.3
  3.9 1.0 %copy-done.3 = bf16[1,64,4096]{2,1,0:T(8,128)(2,1)S(1)} copy-done((bf16[1,64,4096]{2,1,0:T(8,128)(2,1)S(1)}, bf16[1,64,4096]{2,1,0:T(8,128)(2,1)}, u32[]{:S(2)}) %copy-start.3) | copy-done | bytes 524312
  5.0 0.0 copy-start.4
  5.0 1.0 %copy-done.4 = bf16[1,16,128,128]{3,2,1,0:T(8,128)(2,1)S(1)} copy-done((bf16[1,16,128,128]{3,2,1,0:T(8,128)(2,1)S(1)}, bf16[1,16,128,128]{3,2,1,0:T(8,128)(2,1)}, u32[]{:S(2)}) %copy-start.4) | copy-done | bytes 524312
  6.0 0.0 copy-start.5
  6.0 0.9 %copy-done.5 = bf16[1,32,4096]{2,1,0:T(8,128)(2,1)S(1)} copy-done((bf16[1,32,4096]{2,1,0:T(8,128)(2,1)S(1)}, bf16[1,32,4096]{2,1,0:T(8,128)(2,1)}, u32[]{:S(2)}) %copy-start.5) | copy-done | bytes 262168
  7.0 17.8 %shard_map.64 = bf16[32,736]{1,0:T(8,128)(2,1)S(1)} custom-call(bf16[1,32,2,4096]{3,2,1,0:T(2,128)(2,1)S(1)} %copy-done.1, bf16[1,32,2,4096]{3,2,1,0:T(2,128)(2,1)S(1)} %copy-done.2, bf16[1,64,4096]{2,1,0:T(8,128)(2,1)S(1)} %copy-done.3, bf16[1,32,4096]{2,1,0:T(8,128)(2,1)S(1)} %copy-done.5, bf16[1,16,128,128]{3,2,1,0:T(8,128)(2,1)S(1)} %copy-done.4, ...), custom_call_target="tpu_custom_call" | custom-call | tf_op jit(solution)/shard_map/pallas_call | solution.py:230
  24.8 0.6 %copy.8 = bf16[32,736]{1,0:T(8,128)(2,1)} copy(bf16[32,736]{1,0:T(8,128)(2,1)S(1)} %shard_map.64) | data formatting | bytes 94208
Async XLA Ops:
  0.0 1.9 %copy-start = (bf16[736,2048]{1,0:T(8,128)(2,1)S(1)}, bf16[736,2048]{1,0:T(8,128)(2,1)}, u32[]{:S(2)}) copy-start(bf16[736,2048]{1,0:T(8,128)(2,1)} %store_hbm.1) | copy-start | bytes 9043972
  1.9 1.0 %copy-start.1 = (bf16[1,32,2,4096]{3,2,1,0:T(2,128)(2,1)S(1)}, bf16[1,32,2,4096]{3,2,1,0:T(2,128)(2,1)}, u32[]{:S(2)}) copy-start(bf16[1,32,2,4096]{3,2,1,0:T(2,128)(2,1)} %qin_hbm.1) | copy-start | bytes 1572868
  2.9 1.0 %copy-start.2 = (bf16[1,32,2,4096]{3,2,1,0:T(2,128)(2,1)S(1)}, bf16[1,32,2,4096]{3,2,1,0:T(2,128)(2,1)}, u32[]{:S(2)}) copy-start(bf16[1,32,2,4096]{3,2,1,0:T(2,128)(2,1)} %qgr_hbm.1) | copy-start | bytes 1572868
  3.9 1.0 %copy-start.3 = (bf16[1,64,4096]{2,1,0:T(8,128)(2,1)S(1)}, bf16[1,64,4096]{2,1,0:T(8,128)(2,1)}, u32[]{:S(2)}) copy-start(bf16[1,64,4096]{2,1,0:T(8,128)(2,1)} %pin_hbm.1) | copy-start | bytes 1572868
  5.0 1.0 %copy-start.4 = (bf16[1,16,128,128]{3,2,1,0:T(8,128)(2,1)S(1)}, bf16[1,16,128,128]{3,2,1,0:T(8,128)(2,1)}, u32[]{:S(2)}) copy-start(bf16[1,16,128,128]{3,2,1,0:T(8,128)(2,1)} %hess_hbm.1) | copy-start | bytes 1572868
  6.0 0.9 %copy-start.5 = (bf16[1,32,4096]{2,1,0:T(8,128)(2,1)S(1)}, bf16[1,32,4096]{2,1,0:T(8,128)(2,1)}, u32[]{:S(2)}) copy-start(bf16[1,32,4096]{2,1,0:T(8,128)(2,1)} %pout_hbm.1) | copy-start | bytes 786436

commit v2 on v1

--- a/solution.py
+++ b/solution.py
@@ -230,11 +230,11 @@
     return pl.pallas_call(
         functools.partial(kernel, stores, layers, peers_per_step),
         out_shape=jax.ShapeDtypeStruct((own, rows), bf16),
-        in_specs=[pl.BlockSpec(memory_space=pl.ANY)] * 6,
+        in_specs=[pl.BlockSpec(memory_space=pltpu.HBM)] * 6,
         out_specs=pl.BlockSpec(memory_space=pltpu.VMEM),
         scratch_shapes=scratch,
         compiler_params=pltpu.CompilerParams(
-            collective_id=0, has_side_effects=True, vmem_limit_bytes=48 * 2**20
+            collective_id=0, has_side_effects=True, vmem_limit_bytes=64 * 2**20 - 2**17
         ),
     )(query_inputs, query_grads, proj_in, proj_out, hess_inv, store_sketch)
 

time: 25.7 us -> 20.4 us (0.79)
  local copies, waits for them, and re-layouts: 7.59 us -> 1.42 us
  Pallas kernels: 17.8 us -> 18.8 us
    unnamed x13 -> x1, local copies, waits for them, and re-layouts: 7.59 us -> 1.42 us
    pallas_call x1, Pallas kernels: 17.8 us -> 18.8 us  [shards(): pl.pallas_call(functools.partial(kernel, stores, layers, peers_per_step),...]
where the time goes in v2:
time: 20.4 us; the launch traced here: 20.2 us
  Pallas kernels  18.8 us (92%)
  local copies, waits for them, and re-layouts  1.42 us (7%)
    pallas_call x1, Pallas kernels, shards(): pl.pallas_call(functools.partial(kernel, stores, layers, peers_per_step),...  18.8 us
    unnamed x1, local copies, waits for them, and re-layouts  1.42 us

profile of v2, /device:TPU:0, one launch (start us, length us, event | category | flops | bytes accessed | tf_op | source)
XLA Modules:
  0.0 20.2 jit_solution(2305262062563792839)
XLA Ops:
  0.0 18.8 %shard_map.64 = bf16[32,736]{1,0:T(8,128)(2,1)} custom-call(bf16[1,32,2,4096]{3,2,1,0:T(2,128)(2,1)} %qin_hbm.1, bf16[1,32,2,4096]{3,2,1,0:T(2,128)(2,1)} %qgr_hbm.1, bf16[1,64,4096]{2,1,0:T(8,128)(2,1)} %pin_hbm.1, bf16[1,32,4096]{2,1,0:T(8,128)(2,1)} %pout_hbm.1, bf16[1,16,128,128]{3,2,1,0:T(8,128)(2,1)} %hess_hbm.1, bf16[736,2048]{1,0:T(8,128)(2,1)} %store_hbm.1), custom_call_target="tpu_custom_call" | custom-call | tf_op jit(solution)/shard_map/pallas_call | solution.py:230
  18.8 1.4 %copy.8 = bf16[32,736]{1,0:T(8,128)(2,1)} copy(bf16[32,736]{1,0:T(8,128)(2,1)} %shard_map.64) | data formatting | bytes 94208

commit v3 on v2

--- a/solution.py
+++ b/solution.py
@@ -10,6 +10,7 @@
 epsilon = 1e-06
 MESH = pl.DeviceIdType.MESH
 CHUNK = 256
+GROUP = 3
 LANES = 128
 f32, bf16 = jnp.float32, jnp.bfloat16
 
@@ -26,7 +27,7 @@
 
 
 def kernel(
-    stores, layers, peers_per_step,
+    stores, layers, group,
     qin_hbm, qgr_hbm, pin_hbm, pout_hbm, hess_hbm, store_hbm, out_ref,
     qin, qgr, pin, pout, hess, store, mixed, factors, expand, unit, norms, part, got,
     load_sem, fsend_sem, frecv_sem, psend_sem, precv_sem,
@@ -73,6 +74,9 @@
     row = lax.rem(lax.broadcasted_iota(jnp.int32, (depth, LANES), 0), LANES)
     col = lax.broadcasted_iota(jnp.int32, (depth, LANES), 1)
     per_block = blk // k_in
+    pair = 2 if blocks % 2 == 0 else 1
+    step_rows = min(LANES, unit.shape[0])
+    steps = unit.shape[0] // step_rows
     for b in range(blocks):
         hit = row == k_in + b * per_block + col // k_in
         expand[:, b * blk : (b + 1) * blk] = jnp.where(hit, 1.0, 0.0).astype(bf16)
@@ -101,51 +105,70 @@
             src_ref=factors.at[my_store],
             dst_ref=factors.at[my_store],
             send_sem=fsend_sem.at[hop - 1],
-            recv_sem=frecv_sem.at[hop - 1],
+            recv_sem=frecv_sem.at[my_store],
             device_id={"store": lax.rem(my_store + hop, stores)},
             device_id_type=MESH,
         )
 
-    def factor_arrival(hop):
-        source = lax.rem(my_store - hop + stores, stores)
-        return pltpu.make_async_remote_copy(
+    def nearest(k):
+        up = k + (my_store <= k).astype(jnp.int32)
+        down = stores - 1 - k
+        down = down - (down <= my_store).astype(jnp.int32)
+        return jnp.where(2 * my_store < stores, up, down)
+
+    def await_factors(source):
+        pltpu.make_async_remote_copy(
             src_ref=factors.at[source],
             dst_ref=factors.at[source],
-            send_sem=fsend_sem.at[hop - 1],
-            recv_sem=frecv_sem.at[hop - 1],
+            send_sem=fsend_sem.at[0],
+            recv_sem=frecv_sem.at[source],
             device_id={"store": source},
             device_id_type=MESH,
-        )
-
-    for hop in range(1, stores):
+        ).wait_recv()
+
+    def precondition(sources):
+        count = len(sources)
+        joined = [factors[source] for source in sources]
+        joined = joined[0] if count == 1 else jnp.concatenate(joined, axis=0)
+
+        def spread(first, size):
+            value = jnp.dot(joined, expand[:, first : first + size], preferred_element_type=f32)
+            return value.reshape(count, tokens, queries, size)
+
+        features = spread(sketch, blk)
+        total = jnp.zeros((count * queries, blk), f32)
+        for b in range(0, blocks, pair):
+            wide = spread(b * blk, pair * blk)
+            for i in range(pair):
+                outer = jnp.sum(wide[..., i * blk : (i + 1) * blk] * features, axis=1)
+                outer = outer.reshape(count * queries, blk).astype(bf16)
+                precond = contract(outer, hess[b + i])
+                total += precond * precond
+                precond = precond.astype(bf16)
+                for n, source in enumerate(sources):
+                    to = pl.ds(pl.multiple_of(source * queries, queries), queries)
+                    unit[to, (b + i) * blk : (b + i + 1) * blk] = precond[n * queries : (n + 1) * queries]
+        square = jnp.broadcast_to(jnp.sum(total, axis=1, keepdims=True), total.shape) * 0.25
+        for n, source in enumerate(sources):
+            to = pl.ds(pl.multiple_of(source * queries, queries), queries)
+            norms[to, :] = square[n * queries : (n + 1) * queries]
+
+    for hop in range(stores - 1, 0, -1):
         factor_copy(hop).start()
     loads[4].wait()
-    for hop in range(1, stores):
-        factor_arrival(hop).wait_recv()
-
-    step_rows = peers_per_step * queries
-    steps = stores // peers_per_step
-
-    def precondition(step):
-        at = pl.ds(step * peers_per_step, peers_per_step)
-        joined = factors[at].reshape(peers_per_step * tokens * queries, depth)
-
-        def spread(first):
-            value = jnp.dot(joined, expand[:, first : first + blk], preferred_element_type=f32)
-            return value.reshape(peers_per_step, tokens, queries, blk)
-
-        features = spread(sketch)
-        total = jnp.zeros((step_rows, blk), f32)
-        to = pl.ds(pl.multiple_of(step * step_rows, step_rows), step_rows)
-        for b in range(blocks):
-            outer = jnp.sum(spread(b * blk) * features, axis=1)
-            outer = outer.reshape(step_rows, blk).astype(bf16)
-            precond = contract(outer, hess[b])
-            total += precond * precond
-            unit[to, b * blk : (b + 1) * blk] = precond.astype(bf16)
-        norms[to, :] = jnp.broadcast_to(jnp.sum(total, axis=1, keepdims=True), (step_rows, LANES)) * 0.25
-
-    repeat(steps, precondition)
+    precondition([my_store])
+
+    def arrived(step):
+        sources = [nearest(step * group + k) for k in range(group)]
+        for source in sources:
+            await_factors(source)
+        precondition(sources)
+
+    if stores - 1 <= 4:
+        for step in range((stores - 1) // group):
+            arrived(step)
+    else:
+        repeat((stores - 1) // group, arrived)
 
     def part_copy(c, hop):
         peer = lax.rem(my_layer + hop, layers)
@@ -206,7 +229,7 @@
     chunks = -(-(rows + 2) // CHUNK)
     every = queries * stores
     own = every // layers
-    peers_per_step = 4 if stores % 4 == 0 else 1
+    group = GROUP if (stores - 1) % GROUP == 0 else 1
     scratch = [
         pltpu.VMEM((queries, tokens, width), bf16),
         pltpu.VMEM((queries, tokens, width), bf16),
@@ -223,20 +246,25 @@
         pltpu.VMEM((chunks, layers - 1, own, CHUNK), bf16),
         pltpu.SemaphoreType.DMA((5 + chunks,)),
         pltpu.SemaphoreType.DMA((stores - 1,)),
-        pltpu.SemaphoreType.DMA((stores - 1,)),
+        pltpu.SemaphoreType.DMA((stores,)),
         pltpu.SemaphoreType.DMA((chunks, layers - 1)),
         pltpu.SemaphoreType.DMA((chunks, layers - 1)),
     ]
     return pl.pallas_call(
-        functools.partial(kernel, stores, layers, peers_per_step),
-        out_shape=jax.ShapeDtypeStruct((own, rows), bf16),
+        functools.partial(kernel, stores, layers, group),
+        out_shape=pltpu.VMEM((own, rows), bf16),
         in_specs=[pl.BlockSpec(memory_space=pltpu.HBM)] * 6,
         out_specs=pl.BlockSpec(memory_space=pltpu.VMEM),
         scratch_shapes=scratch,
         compiler_params=pltpu.CompilerParams(
-            collective_id=0, has_side_effects=True, vmem_limit_bytes=64 * 2**20 - 2**17
+            collective_id=0, has_side_effects=True, vmem_limit_bytes=48 * 2**20
         ),
-    )(query_inputs, query_grads, proj_in, proj_out, hess_inv, store_sketch)
+    )(
+        *(
+            pltpu.with_memory_space_constraint(x, pltpu.HBM)
+            for x in (query_inputs, query_grads, proj_in, proj_out, hess_inv, store_sketch)
+        )
+    )
 
 
 def solution(mesh):

time: 20.4 us -> 17.9 us (0.88)
  Pallas kernels: 18.8 us -> 17.2 us
  local copies, waits for them, and re-layouts: 1.42 us -> 0.62 us
    pallas_call x1, Pallas kernels: 18.8 us -> 17.2 us  [shards(): pl.pallas_call(functools.partial(kernel, stores, layers, group), out_shap...]
    unnamed x1, local copies, waits for them, and re-layouts: 1.42 us -> 0.62 us
where the time goes in v3:
time: 17.9 us; the launch traced here: 17.8 us
  Pallas kernels  17.2 us (96%)
  local copies, waits for them, and re-layouts  0.62 us (3%)
    pallas_call x1, Pallas kernels, shards(): pl.pallas_call(functools.partial(kernel, stores, layers, group), out_shap...  17.2 us
    unnamed x1, local copies, waits for them, and re-layouts  0.62 us

profile of v3, /device:TPU:0, one launch (start us, length us, event | category | flops | bytes accessed | tf_op | source)
XLA Modules:
  0.0 17.8 jit_solution(8967388485199614570)
XLA Ops:
  0.0 17.2 %shard_map.64 = bf16[32,736]{1,0:T(8,128)(2,1)S(1)} custom-call(bf16[1,32,2,4096]{3,2,1,0:T(2,128)(2,1)} %qin_hbm.1, bf16[1,32,2,4096]{3,2,1,0:T(2,128)(2,1)} %qgr_hbm.1, bf16[1,64,4096]{2,1,0:T(8,128)(2,1)} %pin_hbm.1, bf16[1,32,4096]{2,1,0:T(8,128)(2,1)} %pout_hbm.1, bf16[1,16,128,128]{3,2,1,0:T(8,128)(2,1)} %hess_hbm.1, bf16[736,2048]{1,0:T(8,128)(2,1)} %store_hbm.1), custom_call_target="tpu_custom_call" | custom-call | tf_op jit(solution)/shard_map/pallas_call | solution.py:253
  17.2 0.6 %copy.8 = bf16[32,736]{1,0:T(8,128)(2,1)} copy(bf16[32,736]{1,0:T(8,128)(2,1)S(1)} %shard_map.64) | data formatting | bytes 94208

commit v4 on v3

--- a/solution.py
+++ b/solution.py
@@ -9,7 +9,7 @@
 
 epsilon = 1e-06
 MESH = pl.DeviceIdType.MESH
-CHUNK = 256
+CHUNK = 384
 GROUP = 3
 LANES = 128
 f32, bf16 = jnp.float32, jnp.bfloat16
@@ -94,9 +94,6 @@
         value = mixed[pl.ds(t, queries, stride=tokens), :]
         high = value.astype(bf16)
         factors[my_store, t * queries : (t + 1) * queries, 0:LANES] = high
-        factors[my_store, t * queries : (t + 1) * queries, LANES:] = (
-            value - high.astype(f32)
-        ).astype(bf16)
 
     pl.semaphore_wait(barrier, stores + layers - 2)
 
@@ -137,17 +134,19 @@
 
         features = spread(sketch, blk)
         total = jnp.zeros((count * queries, blk), f32)
+        outers = []
         for b in range(0, blocks, pair):
             wide = spread(b * blk, pair * blk)
             for i in range(pair):
                 outer = jnp.sum(wide[..., i * blk : (i + 1) * blk] * features, axis=1)
-                outer = outer.reshape(count * queries, blk).astype(bf16)
-                precond = contract(outer, hess[b + i])
-                total += precond * precond
-                precond = precond.astype(bf16)
-                for n, source in enumerate(sources):
-                    to = pl.ds(pl.multiple_of(source * queries, queries), queries)
-                    unit[to, (b + i) * blk : (b + i + 1) * blk] = precond[n * queries : (n + 1) * queries]
+                outers.append(outer.reshape(count * queries, blk).astype(bf16))
+        for b in range(blocks):
+            precond = jnp.dot(outers[b], hess[b], preferred_element_type=f32)
+            total += precond * precond
+            precond = precond.astype(bf16)
+            for n, source in enumerate(sources):
+                to = pl.ds(pl.multiple_of(source * queries, queries), queries)
+                unit[to, b * blk : (b + 1) * blk] = precond[n * queries : (n + 1) * queries]
         square = jnp.broadcast_to(jnp.sum(total, axis=1, keepdims=True), total.shape) * 0.25
         for n, source in enumerate(sources):
             to = pl.ds(pl.multiple_of(source * queries, queries), queries)
@@ -238,8 +237,8 @@
         pltpu.VMEM((blocks, blk, blk), bf16),
         pltpu.VMEM((chunks * CHUNK, sketch), bf16),
         pltpu.VMEM((tokens * queries, LANES), f32),
-        pltpu.VMEM((stores, tokens * queries, 2 * LANES), bf16),
-        pltpu.VMEM((2 * LANES, sketch + blk), bf16),
+        pltpu.VMEM((stores, tokens * queries, LANES), bf16),
+        pltpu.VMEM((LANES, sketch + blk), bf16),
         pltpu.VMEM((every, sketch), bf16),
         pltpu.VMEM((every, LANES), f32),
         pltpu.VMEM((chunks, every, CHUNK), bf16),

time: 17.9 us -> 15.7 us (0.88)
  Pallas kernels: 17.2 us -> 14.9 us
    pallas_call x1, Pallas kernels: 17.2 us -> 14.9 us  [shards(): pl.pallas_call(functools.partial(kernel, stores, layers, group), out_shap...]
where the time goes in v4:
time: 15.7 us; the launch traced here: 15.6 us
  Pallas kernels  14.9 us (95%)
  local copies, waits for them, and re-layouts  0.62 us (4%)
    pallas_call x1, Pallas kernels, shards(): pl.pallas_call(functools.partial(kernel, stores, layers, group), out_shap...  14.9 us
    unnamed x1, local copies, waits for them, and re-layouts  0.62 us

profile of v4, /device:TPU:0, one launch (start us, length us, event | category | flops | bytes accessed | tf_op | source)
XLA Modules:
  0.0 15.6 jit_solution(1161954344996536334)
XLA Ops:
  0.0 14.9 %shard_map.64 = bf16[32,736]{1,0:T(8,128)(2,1)S(1)} custom-call(bf16[1,32,2,4096]{3,2,1,0:T(2,128)(2,1)} %qin_hbm.1, bf16[1,32,2,4096]{3,2,1,0:T(2,128)(2,1)} %qgr_hbm.1, bf16[1,64,4096]{2,1,0:T(8,128)(2,1)} %pin_hbm.1, bf16[1,32,4096]{2,1,0:T(8,128)(2,1)} %pout_hbm.1, bf16[1,16,128,128]{3,2,1,0:T(8,128)(2,1)} %hess_hbm.1, bf16[736,2048]{1,0:T(8,128)(2,1)} %store_hbm.1), custom_call_target="tpu_custom_call" | custom-call | tf_op jit(solution)/shard_map/pallas_call | solution.py:252
  14.9 0.6 %copy.8 = bf16[32,736]{1,0:T(8,128)(2,1)} copy(bf16[32,736]{1,0:T(8,128)(2,1)S(1)} %shard_map.64) | data formatting | bytes 94208

commit v5 on v4

--- a/solution.py
+++ b/solution.py
@@ -10,7 +10,7 @@
 epsilon = 1e-06
 MESH = pl.DeviceIdType.MESH
 CHUNK = 384
-GROUP = 3
+GROUP = 1
 LANES = 128
 f32, bf16 = jnp.float32, jnp.bfloat16
 
@@ -152,7 +152,7 @@
             to = pl.ds(pl.multiple_of(source * queries, queries), queries)
             norms[to, :] = square[n * queries : (n + 1) * queries]
 
-    for hop in range(stores - 1, 0, -1):
+    for hop in range(1, stores):
         factor_copy(hop).start()
     loads[4].wait()
     precondition([my_store])

time: 15.7 us -> 15.2 us (0.968)
  Pallas kernels: 14.9 us -> 14.5 us
    pallas_call x1, Pallas kernels: 14.9 us -> 14.5 us  [shards(): pl.pallas_call(functools.partial(kernel, stores, layers, group), out_shap...]
where the time goes in v5:
time: 15.2 us; the launch traced here: 15.1 us
  Pallas kernels  14.5 us (95%)
  local copies, waits for them, and re-layouts  0.62 us (4%)
    pallas_call x1, Pallas kernels, shards(): pl.pallas_call(functools.partial(kernel, stores, layers, group), out_shap...  14.5 us
    unnamed x1, local copies, waits for them, and re-layouts  0.62 us

profile of v5, /device:TPU:0, one launch (start us, length us, event | category | flops | bytes accessed | tf_op | source)
XLA Modules:
  0.0 15.1 jit_solution(3057713435435315162)
XLA Ops:
  0.0 14.5 %shard_map.64 = bf16[32,736]{1,0:T(8,128)(2,1)S(1)} custom-call(bf16[1,32,2,4096]{3,2,1,0:T(2,128)(2,1)} %qin_hbm.1, bf16[1,32,2,4096]{3,2,1,0:T(2,128)(2,1)} %qgr_hbm.1, bf16[1,64,4096]{2,1,0:T(8,128)(2,1)} %pin_hbm.1, bf16[1,32,4096]{2,1,0:T(8,128)(2,1)} %pout_hbm.1, bf16[1,16,128,128]{3,2,1,0:T(8,128)(2,1)} %hess_hbm.1, bf16[736,2048]{1,0:T(8,128)(2,1)} %store_hbm.1), custom_call_target="tpu_custom_call" | custom-call | tf_op jit(solution)/shard_map/pallas_call | solution.py:252
  14.5 0.6 %copy.8 = bf16[32,736]{1,0:T(8,128)(2,1)} copy(bf16[32,736]{1,0:T(8,128)(2,1)S(1)} %shard_map.64) | data formatting | bytes 94208

commit v6 on v5

--- a/solution.py
+++ b/solution.py
@@ -41,6 +41,16 @@
     own = got.shape[2]
     tail = rows - (chunks - 1) * CHUNK
 
+    barrier = pltpu.get_barrier_semaphore()
+    for hop in range(1, stores):
+        pl.semaphore_signal(
+            barrier, inc=1, device_id={"store": lax.rem(my_store + hop, stores)}, device_id_type=MESH
+        )
+    for hop in range(1, layers):
+        pl.semaphore_signal(
+            barrier, inc=1, device_id={"layer": lax.rem(my_layer + hop, layers)}, device_id_type=MESH
+        )
+
     def load(source, target, index):
         copy = pltpu.make_async_copy(source, target, load_sem.at[index])
         copy.start()
@@ -59,22 +69,12 @@
         at = pl.ds(c * CHUNK, size)
         store_loads.append(load(store_hbm.at[at], store.at[at], 5 + c))
 
-    barrier = pltpu.get_barrier_semaphore()
-    for hop in range(1, stores):
-        pl.semaphore_signal(
-            barrier, inc=1, device_id={"store": lax.rem(my_store + hop, stores)}, device_id_type=MESH
-        )
-    for hop in range(1, layers):
-        pl.semaphore_signal(
-            barrier, inc=1, device_id={"layer": lax.rem(my_layer + hop, layers)}, device_id_type=MESH
-        )
-
     depth = expand.shape[0]
     sketch = blocks * blk
     row = lax.rem(lax.broadcasted_iota(jnp.int32, (depth, LANES), 0), LANES)
     col = lax.broadcasted_iota(jnp.int32, (depth, LANES), 1)
     per_block = blk // k_in
-    pair = 2 if blocks % 2 == 0 else 1
+    pair = 1
     step_rows = min(LANES, unit.shape[0])
     steps = unit.shape[0] // step_rows
     for b in range(blocks):

time: 15.2 us -> 15.3 us (level)
  no operation moved by 1% of the time
where the time goes in v6:
time: 15.3 us; the launch traced here: 15.1 us
  Pallas kernels  14.5 us (95%)
  local copies, waits for them, and re-layouts  0.62 us (4%)
    pallas_call x1, Pallas kernels, shards(): pl.pallas_call(functools.partial(kernel, stores, layers, group), out_shap...  14.5 us
    unnamed x1, local copies, waits for them, and re-layouts  0.62 us

profile of v6, /device:TPU:0, one launch (start us, length us, event | category | flops | bytes accessed | tf_op | source)
XLA Modules:
  0.0 15.1 jit_solution(10596209362620595956)
XLA Ops:
  0.0 14.5 %shard_map.64 = bf16[32,736]{1,0:T(8,128)(2,1)S(1)} custom-call(bf16[1,32,2,4096]{3,2,1,0:T(2,128)(2,1)} %qin_hbm.1, bf16[1,32,2,4096]{3,2,1,0:T(2,128)(2,1)} %qgr_hbm.1, bf16[1,64,4096]{2,1,0:T(8,128)(2,1)} %pin_hbm.1, bf16[1,32,4096]{2,1,0:T(8,128)(2,1)} %pout_hbm.1, bf16[1,16,128,128]{3,2,1,0:T(8,128)(2,1)} %hess_hbm.1, bf16[736,2048]{1,0:T(8,128)(2,1)} %store_hbm.1), custom_call_target="tpu_custom_call" | custom-call | tf_op jit(solution)/shard_map/pallas_call | solution.py:252
  14.5 0.6 %copy.8 = bf16[32,736]{1,0:T(8,128)(2,1)} copy(bf16[32,736]{1,0:T(8,128)(2,1)S(1)} %shard_map.64) | data formatting | bytes 94208
